TPU v7x, 32 devices: a whole 2x2x4 slice. The times are simulated.
32 devices in a mesh: parts: 2 (over y), blk: 4 (over z), op: 4 (over x, core).
Axes of the slice: x: 2, y: 2, z: 4, core: 2. Of those that a mesh axis runs over, the one named last changes fastest.
Arguments:
- psi: bfloat16 [16, 8, 128, 128], P(('parts', 'blk')), parts along dimension 0, may hold values from -6 to 6
- left_ops: bfloat16 [32, 8, 128, 128], P(('parts', 'op'), 'blk'), parts along dimension 0, may hold values from -0.5 to 0.5
- right_ops: bfloat16 [32, 8, 128, 128], P(('parts', 'op'), 'blk'), parts along dimension 0, may hold values from -0.1875 to 0.1875
- term_blocks: int32 [32, 8], P(('parts', 'op')), parts along dimension 0, may hold values from 0 to 1, as said below
- left_sizes: int32 [16], P('parts'), parts along dimension 0, may hold values from 1 to 128
- right_sizes: int32 [16], P('parts'), parts along dimension 0, may hold values from 1 to 128
Outputs:
- sigma: bfloat16 [16, 8, 128, 128], P(('parts', 'blk'), 'op'), parts along dimension 0
There are 2 independent parts, one for each index of `parts`. A program takes and returns all parts, laid end to end along the dimension named above; each array names one. Nothing has to cross between parts.
Inputs may be any that keep to these rules, and one draw needn't show every extreme that they name: `term_blocks`: terms come in consecutive groups of 4; within every group, exactly 2 terms act on each left sector.
All inputs are finite; a program needn't handle non-finite values.
Results may differ from a plain program's by a relative error of at most 0.0095.
Values may be sent and summed in bfloat16 or wider, within the bound.
No kernel may reach another device: no remote copies, remote signals or barrier semaphores. Data moves between devices by JAX's collectives and lax.ppermute only.
A program may use at most 128 MiB of HBM per device.

v0:
```python
import jax
import jax.numpy as jnp
from jax import lax
from jax.sharding import PartitionSpec as P


def shards(psi, left_ops, right_ops, term_blocks, left_sizes, right_sizes):
    sectors_here = psi.shape[0]
    tile_size = psi.shape[2]
    left_first = lax.axis_index("blk") * sectors_here
    positions = lax.broadcasted_iota(jnp.int32, (tile_size,), 0)
    left_local = lax.dynamic_slice_in_dim(left_sizes, left_first, sectors_here)
    left_keep = positions[None, :] < left_local[:, None]
    right_keep = positions[None, :] < right_sizes[:, None]
    keep_mask = (left_keep[:, None, :, None] & right_keep[None, :, None, :]).astype(jnp.bfloat16)
    masked = psi * keep_mask
    acting_count = left_ops.shape[0] // 2
    order = jnp.argsort(1 - term_blocks, axis=0, stable=True)[:acting_count]
    ids_local = lax.dynamic_slice_in_dim(order, left_first, sectors_here, 1)
    sector_index = lax.broadcasted_iota(jnp.int32, (acting_count, sectors_here), 1)
    picked = left_ops[ids_local, sector_index]
    applied = jnp.einsum(
        "kaim,abmj->kabij", picked, masked, preferred_element_type=jnp.float32
    ).astype(jnp.bfloat16)
    arrived = lax.all_to_all(applied, "blk", split_axis=2, concat_axis=1, tiled=True)
    right_picked = right_ops[order]
    partial_value = jnp.einsum(
        "kabij,kablj->bail", arrived, right_picked, preferred_element_type=jnp.float32
    )
    summed = lax.psum_scatter(
        partial_value.astype(jnp.bfloat16), "op", scatter_dimension=1, tiled=True
    ).astype(jnp.float32)
    row_count = summed.shape[1]
    op_first = lax.axis_index("op") * row_count
    left_share = lax.dynamic_slice_in_dim(left_sizes, op_first, row_count)
    right_local = lax.dynamic_slice_in_dim(right_sizes, left_first, sectors_here)
    rows_keep = positions[None, :] < left_share[:, None]
    cols_keep = positions[None, :] < right_local[:, None]
    out_keep = (cols_keep[:, None, None, :] & rows_keep[None, :, :, None]).astype(jnp.float32)
    return (summed * out_keep).astype(jnp.bfloat16)


def solution(mesh):
    in_specs = (
        P(("parts", "blk"), None, None, None),
        P(("parts", "op"), "blk", None, None),
        P(("parts", "op"), "blk", None, None),
        P(("parts", "op"), None),
        P("parts"),
        P("parts"),
    )
    out_specs = P(("parts", "blk"), "op", None, None)
    return jax.shard_map(shards, mesh=mesh, in_specs=in_specs, out_specs=out_specs, check_vma=False)
```

profile of v0, /device:TPU:0, one launch (start us, length us, event | category | flops | bytes accessed | tf_op | source)
XLA Modules:
  0.0 88.8 jit_solution(15361863382786427983)
XLA Ops:
  6.5 0.8 fusion.14
  7.3 0.1 iota_compare_fusion.1
  7.4 0.7 broadcast_subtract_fusion
  8.1 0.6 sort.17
  8.7 0.1 fusion.12
  8.8 0.1 reshape.86
  8.9 0.7 iota_compare_fusion
  9.6 1.5 %gather_fusion = bf16[4,128,128]{2,1,0:T(8,128)(2,1)S(1)} fusion(bf16[4,2,128,128]{3,2,1,0:T(8,128)(2,1)} %param.7, s32[4]{0:T(128)S(1)} %reshape.86), kind=kCustom, calls=%fused_computation | custom fusion | bytes 262176 | tf_op jit(solution)/shard_map/gather | solution.py:21
  11.2 1.6 %fusion = bf16[2,2,8,128,128]{3,4,0,2,1:T(8,128)(2,1)S(1)} fusion(bf16[2,8,128,128]{3,2,1,0:T(8,128)(2,1)} %param.6, pred[8,128]{1,0:T(8,128)(4,1)S(1)} %iota_compare_fusion, pred[2,128]{1,0:T(4,128)(4,1)S(1)} %iota_compare_fusion.1, bf16[2,2,128,128,1]{3,2,1,0,4:T(8,128)(2,1)S(1)} %bitcast.37), kind=kOutput, calls=%fused_computation.3 | convolution fusion | flops 135266304 | bytes 1705216 | tf_op jit(solution)/shard_map/kaim,abmj->kabij/dot_general | solution.py:22
  12.8 1.1 %copy.13 = bf16[2,2,8,128,128]{3,4,0,1,2:T(8,128)(2,1)} copy(bf16[2,2,8,128,128]{3,4,0,2,1:T(8,128)(2,1)S(1)} %fusion) | data formatting | bytes 2097152 | tf_op jit(solution)/shard_map/convert_element_type | solution.py:24
  13.8 6.3 %all-to-all-start = ((bf16[2,2,8,128,128]{3,4,0,1,2:T(8,128)(2,1)}), bf16[2,2,8,128,128]{3,4,0,1,2:T(8,128)(2,1)S(1)}, u32[]{:S(2)}, u32[]{:S(2)}) async-start(bf16[2,2,8,128,128]{3,4,0,1,2:T(8,128)(2,1)} %copy.13), calls=%async_computation | async-start | bytes 2097152 | tf_op jit(solution)/shard_map/all_to_all | solution.py:25
  20.2 0.1 reshape.94
  20.3 0.7 gather_fusion.1
  21.0 24.9 %all-to-all-done = bf16[2,2,8,128,128]{3,4,0,1,2:T(8,128)(2,1)S(1)} async-done(((bf16[2,2,8,128,128]{3,4,0,1,2:T(8,128)(2,1)}), bf16[2,2,8,128,128]{3,4,0,1,2:T(8,128)(2,1)S(1)}, u32[]{:S(2)}, u32[]{:S(2)}) %all-to-all-start) | async-done | bytes 1048608 | tf_op jit(solution)/shard_map/all_to_all | solution.py:25
  45.9 0.7 copy.14
  46.6 0.0 copy-start.2
  46.6 1.2 %fusion.1 = bf16[2,8,128,128]{3,2,1,0:T(8,128)(2,1)} fusion(bf16[2,8,2,128,128]{4,3,0,1,2:T(8,128)(2,1)S(1)} %bitcast.35, bf16[2,8,2,128,128]{4,3,2,1,0:T(8,128)(2,1)S(1)} %bitcast.36), kind=kOutput, calls=%fused_computation.5 | convolution fusion | flops 134479872 | bytes 2621440 | tf_op jit(solution)/shard_map/kabij,kablj->bail/dot_general | solution.py:27
  47.8 0.0 all-reduce.3.cloned.1.call-update
  47.8 0.1 iota_compare_fusion.2
  47.9 0.1 dynamic_slice.12
  48.0 0.6 dynamic-slice
  49.2 0.1 iota_compare_fusion.3
  49.3 31.0 %all-reduce.3.cloned.1.call-done = bf16[2,8,128,128]{3,2,1,0:T(8,128)(2,1)} async-done(((bf16[2,8,128,128]{3,2,1,0:T(8,128)(2,1)}), bf16[2,8,128,128]{3,2,1,0:T(8,128)(2,1)}) %all-reduce.3.cloned.1.call-update) | async-done | bytes 524304
  80.3 1.7 %select_convert_fusion = bf16[2,2,128,128]{3,2,1,0:T(8,128)(2,1)} fusion(bf16[2,8,128,128]{3,2,1,0:T(8,128)(2,1)} %all-reduce.3.cloned.1.call-done, u32[]{:T(128)S(6)} %multiply.1, pred[2,128]{1,0:T(4,128)(4,1)S(1)} %iota_compare_fusion.2, pred[2,128]{1,0:T(4,128)(4,1)S(1)} %iota_compare_fusion.3), kind=kLoop, calls=%fused_computation.11 | loop fusion | flops 262144 | bytes 262660 | tf_op jit(solution)/shard_map/convert_element_type | solution.py:40
  (9 shorter events, 0.0 us)
Async XLA Ops:
  6.5 13.7 %copy-start = (bf16[4,2,128,128]{3,2,1,0:T(8,128)(2,1)S(1)}, bf16[4,2,128,128]{3,2,1,0:T(8,128)(2,1)}, u32[]{:S(2)}) copy-start(bf16[4,2,128,128]{3,2,1,0:T(8,128)(2,1)} %param.8) | copy-start | bytes 786436
  13.8 32.0 %all-to-all-start = ((bf16[2,2,8,128,128]{3,4,0,1,2:T(8,128)(2,1)}), bf16[2,2,8,128,128]{3,4,0,1,2:T(8,128)(2,1)S(1)}, u32[]{:S(2)}, u32[]{:S(2)}) async-start(bf16[2,2,8,128,128]{3,4,0,1,2:T(8,128)(2,1)} %copy.13), calls=%async_computation | async-start | bytes 2097152 | tf_op jit(solution)/shard_map/all_to_all | solution.py:25
  20.2 60.1 %all-reduce.3.cloned.1.call-start = ((), (), s32[]{:S(2)}) async-start(), calls=%async_computation.1 | async-start | bytes 1048576
  46.5 1.4 %copy-start.1 = (s32[8]{0:T(128)S(1)}, s32[8]{0:T(128)}, u32[]{:S(2)}) copy-start(s32[8]{0:T(128)} %param.11) | copy-start | bytes 100
  46.6 1.4 %copy-start.2 = (u32[32]{0:T(128)S(1)}, u32[32]{0:T(128)}, u32[]{:S(2)}) copy-start(u32[32]{0:T(128)} %constant.46) | copy-start | bytes 388
Sparse Core Ops, SparseCore 0:
  48.0 32.2 all-reduce.2
where the time goes:
time: 89.1 us; the launch traced here: 88.8 us
  waiting for transfers between devices  55.9 us (63%)
  between operations  14.1 us (16%)
  starting transfers between devices  6.32 us (7%)
  local copies, waits for them, and re-layouts  5.63 us (6%)
  other arithmetic  4.02 us (5%)
  matrix products  2.87 us (3%)
    unnamed x2, waiting for transfers between devices  31 us
    all_to_all x1, waiting for transfers between devices, shards(): lax.all_to_all(applied, 'blk', split_axis=2, concat_axis=1, tiled=True)  24.9 us
    all_to_all x1, starting transfers between devices, shards(): lax.all_to_all(applied, 'blk', split_axis=2, concat_axis=1, tiled=True)  6.31 us
  transfers between devices with their start and end apart: 2, of which 2 were waited for; matrix products, arithmetic and copies ran while one was open for 2% of the time, Pallas kernels for 0%

commit v1 on v0

--- a/solution.py
+++ b/solution.py
@@ -1,10 +1,158 @@
+import functools
+
 import jax
 import jax.numpy as jnp
 from jax import lax
+from jax.experimental import pallas as pl
+from jax.experimental.pallas import tpu as pltpu
 from jax.sharding import PartitionSpec as P
 
-
-def shards(psi, left_ops, right_ops, term_blocks, left_sizes, right_sizes):
+ANY = pl.BlockSpec(memory_space=pl.ANY)
+SMEM = pl.BlockSpec(memory_space=pltpu.SMEM)
+VMEM = pl.BlockSpec(memory_space=pltpu.VMEM)
+PARAMS = pltpu.CompilerParams(vmem_limit_bytes=32 * 1024 * 1024)
+ID_ROWS = 16
+PSI_STEP = (0, 2, 1, 3)
+
+
+def acting_terms(blocks_ref, sector):
+    first = jnp.int32(0)
+    second = jnp.int32(0)
+    for term in reversed(range(blocks_ref.shape[0])):
+        acts = blocks_ref[term, sector] > 0
+        second = jnp.where(acts, first, second)
+        first = jnp.where(acts, term, first)
+    return first, second
+
+
+def pack_kernel(blocks_ref, psi_ref, left_ref, left_out, psi_out, sem):
+    here = lax.axis_index("blk")
+    mine = lax.axis_index("op")
+    sectors, tile = psi_ref.shape[0], psi_ref.shape[-1]
+    distance = jnp.int32(0)
+    for index, step in enumerate(PSI_STEP):
+        distance = jnp.where(mine == index, step, distance)
+    there = jnp.bitwise_xor(here, distance)
+    copies = [
+        pltpu.make_async_copy(psi_ref.at[:, pl.ds(there * sectors, sectors)], psi_out, sem.at[0])
+    ]
+    row = lax.broadcasted_iota(jnp.int32, (ID_ROWS, tile), 0)
+    ids = jnp.zeros((ID_ROWS, tile), jnp.float32)
+    for local in range(sectors):
+        for slot, term in enumerate(acting_terms(blocks_ref, here * sectors + local)):
+            place = 2 * local + slot
+            copies.append(
+                pltpu.make_async_copy(
+                    left_ref.at[term, local],
+                    left_out.at[pl.ds(place * tile, tile)],
+                    sem.at[len(copies)],
+                )
+            )
+            ids = jnp.where(row == place, term.astype(jnp.float32), ids)
+    for copy in copies:
+        copy.start()
+    left_out[pl.ds(2 * sectors * tile, ID_ROWS)] = ids.astype(jnp.bfloat16)
+    for copy in copies:
+        copy.wait()
+
+
+def apply_kernel(n, lsize_ref, rsize_ref, psi_ref, *rest):
+    lefts, rights, out_ref = rest[:n], rest[n : 2 * n], rest[2 * n]
+    right_all, sem = rest[2 * n + 1 :]
+    here = lax.axis_index("blk")
+    mine = lax.axis_index("op")
+    sectors, tile = out_ref.shape[0], out_ref.shape[-1]
+    terms = right_all.shape[1]
+    copies = [
+        pltpu.make_async_copy(rights[r], right_all.at[jnp.bitwise_xor(here, r)], sem.at[r])
+        for r in range(n)
+    ]
+    for copy in copies:
+        copy.start()
+    rows = lax.broadcasted_iota(jnp.int32, (tile, tile), 0)
+    lanes = lax.broadcasted_iota(jnp.int32, (tile, tile), 1)
+    applied = []
+    for a in range(sectors):
+        height = lsize_ref[mine * sectors + a]
+        cut = []
+        for b in range(sectors):
+            keep = (rows < height) & (lanes < rsize_ref[here * sectors + b])
+            cut.append(jnp.where(keep, psi_ref[a, b].astype(jnp.float32), 0.0).astype(jnp.bfloat16))
+        block = jnp.concatenate(cut, axis=1)
+        applied.append([])
+        for s in range(n):
+            ops = lefts[s][pl.ds(2 * a * tile, 2 * tile)]
+            both = jnp.dot(ops, block, preferred_element_type=jnp.float32).astype(jnp.bfloat16)
+            applied[a] += [both[:tile], both[tile:]]
+    for copy in copies:
+        copy.wait()
+    ids = [lefts[s][pl.ds(2 * sectors * tile, ID_ROWS)].astype(jnp.float32) for s in range(n)]
+    for a in range(sectors):
+        height = lsize_ref[mine * sectors + a]
+        for b in range(sectors):
+            picked = []
+            for s in range(n):
+                for slot in range(2):
+                    place = 2 * a + slot
+                    term = jnp.broadcast_to(ids[s][place : place + 1], (tile, tile))
+                    block = right_all[s, 0, b].astype(jnp.float32)
+                    for t in range(1, terms):
+                        block = jnp.where(term == t, right_all[s, t, b].astype(jnp.float32), block)
+                    picked.append(block.astype(jnp.bfloat16))
+            column = [x[:, b * tile : (b + 1) * tile] for x in applied[a]]
+            total = lax.dot_general(
+                jnp.concatenate(column, axis=1),
+                jnp.concatenate(picked, axis=1),
+                (((1,), (1,)), ((), ())),
+                preferred_element_type=jnp.float32,
+            )
+            keep = (rows < height) & (lanes < rsize_ref[here * sectors + b])
+            out_ref[b, a] = jnp.where(keep, total, 0.0).astype(jnp.bfloat16)
+
+
+def shards(n, psi, left_ops, right_ops, term_blocks, left_sizes, right_sizes):
+    sectors, tile = psi.shape[0], psi.shape[-1]
+    block = functools.partial(jax.ShapeDtypeStruct, dtype=jnp.bfloat16)
+
+    def over_op(array, step):
+        return lax.ppermute(array, "op", [(o, o ^ step) for o in range(n)])
+
+    def over_both(array, target):
+        pairs = []
+        for z in range(n):
+            for o in range(n):
+                to_z, to_o = target(z, o)
+                pairs.append((z * n + o, to_z * n + to_o))
+        return lax.ppermute(array, ("blk", "op"), pairs)
+
+    left_sent, psi_sent = pl.pallas_call(
+        pack_kernel,
+        out_shape=[block((2 * sectors * tile + ID_ROWS, tile)), block((sectors, sectors, tile, tile))],
+        in_specs=[SMEM, ANY, ANY],
+        out_specs=[VMEM, VMEM],
+        scratch_shapes=[pltpu.SemaphoreType.DMA((2 * sectors + 1,))],
+        compiler_params=PARAMS,
+        name="pack",
+    )(term_blocks, psi, left_ops)
+    across = over_op(right_ops, 2)
+    rights = [right_ops, over_op(right_ops, 1), across, over_op(across, 1)]
+    lefts = [over_both(left_sent, lambda z, o: (z ^ o ^ s, z)) for s in range(n)]
+    psi_here = over_both(psi_sent, lambda z, o: (z ^ PSI_STEP[o], z))
+    return pl.pallas_call(
+        functools.partial(apply_kernel, n),
+        out_shape=block((sectors, sectors, tile, tile)),
+        in_specs=[SMEM] * 2 + [VMEM] * (1 + n) + [ANY] * n,
+        out_specs=VMEM,
+        scratch_shapes=[
+            pltpu.VMEM((n,) + right_ops.shape, jnp.bfloat16),
+            pltpu.SemaphoreType.DMA((n,)),
+        ],
+        compiler_params=PARAMS,
+        name="apply",
+    )(left_sizes, right_sizes, psi_here, *lefts, *rights)
+
+
+def wide_shards(psi, left_ops, right_ops, term_blocks, left_sizes, right_sizes):
     sectors_here = psi.shape[0]
     tile_size = psi.shape[2]
     left_first = lax.axis_index("blk") * sectors_here
@@ -50,4 +198,6 @@
         P("parts"),
     )
     out_specs = P(("parts", "blk"), "op", None, None)
-    return jax.shard_map(shards, mesh=mesh, in_specs=in_specs, out_specs=out_specs, check_vma=False)
+    nz, no = mesh.shape["blk"], mesh.shape["op"]
+    body = functools.partial(shards, nz) if nz == no == 4 else wide_shards
+    return jax.shard_map(body, mesh=mesh, in_specs=in_specs, out_specs=out_specs, check_vma=False)

time: 89.1 us -> 36.8 us (0.41)
  the two profiles are of different devices: /device:TPU:0 before, /device:TPU:11 now
where the time goes in v1:
time: 36.8 us; the launch traced here: 36.5 us
  starting transfers between devices  25.1 us (68%)
  waiting for transfers between devices  5.31 us (14%)
  Pallas kernels  3.35 us (9%)
  local copies, waits for them, and re-layouts  2.69 us (7%)
    ppermute x5, starting transfers between devices, over_both(): return lax.ppermute(array, ('blk', 'op'), pairs)  22.6 us
    ppermute x5, waiting for transfers between devices, over_both(): return lax.ppermute(array, ('blk', 'op'), pairs)  5.3 us
    unnamed x12, local copies, waits for them, and re-layouts  2.69 us
    ppermute x3, starting transfers between devices, over_op(): return lax.ppermute(array, 'op', [(o, o ^ step) for o in range(n)])  2.49 us
    pallas_call x1, Pallas kernels, shards(): pl.pallas_call(functools.partial(apply_kernel, n), out_shape=block((secto...  2.45 us
    pallas_call x1, Pallas kernels, shards(): pl.pallas_call(pack_kernel, out_shape=[block((2 * sectors * tile + ID_ROW...  0.91 us
  transfers between devices with their start and end apart: 8, of which 2 were waited for; matrix products, arithmetic and copies ran while one was open for 0% of the time, Pallas kernels for 2%

profile of v1, /device:TPU:11, one launch (start us, length us, event | category | flops | bytes accessed | tf_op | source)
XLA Modules:
  0.0 36.5 jit_solution(2892865814385184098)
XLA Ops:
  0.0 0.3 collective-permute-start.6
  0.3 1.0 %copy-done = bf16[2,8,128,128]{3,2,1,0:T(8,128)(2,1)S(1)} copy-done((bf16[2,8,128,128]{3,2,1,0:T(8,128)(2,1)S(1)}, bf16[2,8,128,128]{3,2,1,0:T(8,128)(2,1)}, u32[]{:S(2)}) %copy-start) | copy-done | bytes 524312
  1.3 0.9 %copy-done.1 = bf16[4,2,128,128]{3,2,1,0:T(8,128)(2,1)S(1)} copy-done((bf16[4,2,128,128]{3,2,1,0:T(8,128)(2,1)S(1)}, bf16[4,2,128,128]{3,2,1,0:T(8,128)(2,1)}, u32[]{:S(2)}) %copy-start.1) | copy-done | bytes 262168
  2.3 0.7 %copy-done.3 = s32[4,8]{1,0:T(4,128)S(1)} copy-done((s32[4,8]{1,0:T(4,128)S(1)}, s32[4,8]{1,0:T(4,128)}, u32[]{:S(2)}) %copy-start.3) | copy-done | bytes 152
  2.9 0.9 %pack.1 = (bf16[528,128]{1,0:T(8,128)(2,1)S(1)}, bf16[2,2,128,128]{3,2,1,0:T(8,128)(2,1)S(1)}) custom-call(s32[4,8]{1,0:T(4,128)S(1)} %copy-done.3, bf16[2,8,128,128]{3,2,1,0:T(8,128)(2,1)S(1)} %copy-done, bf16[4,2,128,128]{3,2,1,0:T(8,128)(2,1)S(1)} %copy-done.1), custom_call_target="tpu_custom_call" | custom-call | tf_op jit(solution)/shard_map/pack/pallas_call | solution.py:128
  3.8 0.0 copy-start.4
  3.9 0.0 copy-start.5
  3.9 3.1 %collective-permute-start.4 = (bf16[528,128]{1,0:T(8,128)(2,1)S(1)}, bf16[528,128]{1,0:T(8,128)(2,1)S(1)}, u32[]{:S(2)}, u32[]{:S(2)}) collective-permute-start(bf16[528,128]{1,0:T(8,128)(2,1)S(1)} %get-tuple-element.8), channel_id=1, source_target_pairs={{0,12},{1,8},{2,4},{3,0},{4,9},{5,13},{6,1},{7,5},{8,6},{9,2},{10,... | collective-permute-start | bytes 405512 | tf_op jit(solution)/shard_map/ppermute | solution.py:126
  7.0 3.3 %collective-permute-start = (bf16[2,2,128,128]{3,2,1,0:T(8,128)(2,1)S(1)}, bf16[2,2,128,128]{3,2,1,0:T(8,128)(2,1)S(1)}, u32[]{:S(2)}, u32[]{:S(2)}) collective-permute-start(bf16[2,2,128,128]{3,2,1,0:T(8,128)(2,1)S(1)} %get-tuple-element.7), channel_id=1, source_target_pairs={{0,0},{1,8},{2,4},{3,12},{4,5},{5,13},{6,1},{7,9},{8,10},{9,2},{10... | collective-permute-start | bytes 393224 | tf_op jit(solution)/shard_map/ppermute | solution.py:126
  10.3 0.0 copy-done.2
  10.3 2.1 %collective-permute-start.5 = (bf16[4,2,128,128]{3,2,1,0:T(8,128)(2,1)S(1)}, bf16[4,2,128,128]{3,2,1,0:T(8,128)(2,1)S(1)}, u32[]{:S(2)}, u32[]{:S(2)}) collective-permute-start(bf16[4,2,128,128]{3,2,1,0:T(8,128)(2,1)S(1)} %copy-done.2), channel_id=1, source_target_pairs={{0,1},{1,0},{2,3},{3,2},{4,5},{5,4},{6,7},{7,6},{8,9},{9,8},{10,11... | collective-permute-start | bytes 786440 | tf_op jit(solution)/shard_map/ppermute | solution.py:118
  12.4 0.0 collective-permute-done.6.rest_6_
  12.4 0.1 collective-permute-start.7
  12.5 2.3 %collective-permute-start.3 = (bf16[528,128]{1,0:T(8,128)(2,1)S(1)}, bf16[528,128]{1,0:T(8,128)(2,1)S(1)}, u32[]{:S(2)}, u32[]{:S(2)}) collective-permute-start(bf16[528,128]{1,0:T(8,128)(2,1)S(1)} %get-tuple-element.8), channel_id=1, source_target_pairs={{0,8},{1,12},{2,0},{3,4},{4,13},{5,9},{6,5},{7,1},{8,2},{9,6},{10,... | collective-permute-start | bytes 405512 | tf_op jit(solution)/shard_map/ppermute | solution.py:126
  14.9 0.0 collective-permute-done.psi_ref
  14.9 11.9 %collective-permute-start.2 = (bf16[528,128]{1,0:T(8,128)(2,1)S(1)}, bf16[528,128]{1,0:T(8,128)(2,1)S(1)}, u32[]{:S(2)}, u32[]{:S(2)}) collective-permute-start(bf16[528,128]{1,0:T(8,128)(2,1)S(1)} %get-tuple-element.8), channel_id=1, source_target_pairs={{0,4},{1,0},{2,12},{3,8},{4,1},{5,5},{6,9},{7,13},{8,14},{9,10},{1... | collective-permute-start | bytes 405512 | tf_op jit(solution)/shard_map/ppermute | solution.py:126
  26.8 0.0 collective-permute-done.4.rest_3_
  26.8 1.9 %collective-permute-start.1 = (bf16[528,128]{1,0:T(8,128)(2,1)S(1)}, bf16[528,128]{1,0:T(8,128)(2,1)S(1)}, u32[]{:S(2)}, u32[]{:S(2)}) collective-permute-start(bf16[528,128]{1,0:T(8,128)(2,1)S(1)} %get-tuple-element.8), channel_id=1, source_target_pairs={{0,0},{1,4},{2,8},{3,12},{4,5},{5,1},{6,13},{7,9},{8,10},{9,14},{1... | collective-permute-start | bytes 405512 | tf_op jit(solution)/shard_map/ppermute | solution.py:126
  28.8 0.0 collective-permute-done.3.rest_2_
  28.8 0.5 %collective-permute-done.2.rest_1_ = bf16[528,128]{1,0:T(8,128)(2,1)S(1)} collective-permute-done((bf16[528,128]{1,0:T(8,128)(2,1)S(1)}, bf16[528,128]{1,0:T(8,128)(2,1)S(1)}, u32[]{:S(2)}, u32[]{:S(2)}) %collective-permute-start.2) | collective-permute-done | bytes 135200 | tf_op jit(solution)/shard_map/ppermute | solution.py:126
  29.3 4.8 %collective-permute-done.1.rest_0_ = bf16[528,128]{1,0:T(8,128)(2,1)S(1)} collective-permute-done((bf16[528,128]{1,0:T(8,128)(2,1)S(1)}, bf16[528,128]{1,0:T(8,128)(2,1)S(1)}, u32[]{:S(2)}, u32[]{:S(2)}) %collective-permute-start.1) | collective-permute-done | bytes 135200 | tf_op jit(solution)/shard_map/ppermute | solution.py:126
  34.1 0.0 collective-permute-done.5.rest_5_
  34.1 0.0 collective-permute-done.7.rest_7_
  34.1 2.4 %apply.1 = bf16[2,2,128,128]{3,2,1,0:T(8,128)(2,1)} custom-call(s32[8]{0:T(128)S(1)} %copy-done.4, s32[8]{0:T(128)S(1)} %copy-done.5, bf16[2,2,128,128]{3,2,1,0:T(8,128)(2,1)S(1)} %collective-permute-done.psi_ref, bf16[528,128]{1,0:T(8,128)(2,1)S(1)} %collective-permute-done.1.rest_0_, bf16[528,128]{1,0:T(8,128)(2,1)S(1)} %collective-permute-done.2.rest_1_, ...), custom_call_target="tpu_custom_call" | custom-call | tf_op jit(solution)/shard_map/apply/pallas_call | solution.py:141
  (6 shorter events, 0.0 us)
Async XLA Ops:
  0.0 12.4 %collective-permute-start.6 = (bf16[4,2,128,128]{3,2,1,0:T(8,128)(2,1)}, bf16[4,2,128,128]{3,2,1,0:T(8,128)(2,1)S(1)}, u32[]{:S(2)}, u32[]{:S(2)}) collective-permute-start(bf16[4,2,128,128]{3,2,1,0:T(8,128)(2,1)} %rest_4_.1), channel_id=1, source_target_pairs={{0,2},{1,3},{2,0},{3,1},{4,6},{5,7},{6,4},{7,5},{8,10},{9,11},{10,... | collective-permute-start | bytes 786440 | tf_op jit(solution)/shard_map/ppermute | solution.py:118
  0.3 1.0 %copy-start = (bf16[2,8,128,128]{3,2,1,0:T(8,128)(2,1)S(1)}, bf16[2,8,128,128]{3,2,1,0:T(8,128)(2,1)}, u32[]{:S(2)}) copy-start(bf16[2,8,128,128]{3,2,1,0:T(8,128)(2,1)} %psi_ref.1) | copy-start | bytes 1572868
  1.3 0.9 %copy-start.1 = (bf16[4,2,128,128]{3,2,1,0:T(8,128)(2,1)S(1)}, bf16[4,2,128,128]{3,2,1,0:T(8,128)(2,1)}, u32[]{:S(2)}) copy-start(bf16[4,2,128,128]{3,2,1,0:T(8,128)(2,1)} %left_ref.1) | copy-start | bytes 786436
  2.2 0.7 %copy-start.3 = (s32[4,8]{1,0:T(4,128)S(1)}, s32[4,8]{1,0:T(4,128)}, u32[]{:S(2)}) copy-start(s32[4,8]{1,0:T(4,128)} %blocks_ref.1) | copy-start | bytes 388
  2.9 7.3 %copy-start.2 = (bf16[4,2,128,128]{3,2,1,0:T(8,128)(2,1)S(1)}, bf16[4,2,128,128]{3,2,1,0:T(8,128)(2,1)}, u32[]{:S(2)}) copy-start(bf16[4,2,128,128]{3,2,1,0:T(8,128)(2,1)} %rest_4_.1) | copy-start | bytes 786436
  3.8 30.2 %copy-start.4 = (s32[8]{0:T(128)S(1)}, s32[8]{0:T(128)}, u32[]{:S(2)}) copy-start(s32[8]{0:T(128)} %lsize_ref.1) | copy-start | bytes 100
  3.9 30.2 %copy-start.5 = (s32[8]{0:T(128)S(1)}, s32[8]{0:T(128)}, u32[]{:S(2)}) copy-start(s32[8]{0:T(128)} %rsize_ref.1) | copy-start | bytes 100
  3.9 23.0 %collective-permute-start.4 = (bf16[528,128]{1,0:T(8,128)(2,1)S(1)}, bf16[528,128]{1,0:T(8,128)(2,1)S(1)}, u32[]{:S(2)}, u32[]{:S(2)}) collective-permute-start(bf16[528,128]{1,0:T(8,128)(2,1)S(1)} %get-tuple-element.8), channel_id=1, source_target_pairs={{0,12},{1,8},{2,4},{3,0},{4,9},{5,13},{6,1},{7,5},{8,6},{9,2},{10,... | collective-permute-start | bytes 405512 | tf_op jit(solution)/shard_map/ppermute | solution.py:126
  7.0 7.9 %collective-permute-start = (bf16[2,2,128,128]{3,2,1,0:T(8,128)(2,1)S(1)}, bf16[2,2,128,128]{3,2,1,0:T(8,128)(2,1)S(1)}, u32[]{:S(2)}, u32[]{:S(2)}) collective-permute-start(bf16[2,2,128,128]{3,2,1,0:T(8,128)(2,1)S(1)} %get-tuple-element.7), channel_id=1, source_target_pairs={{0,0},{1,8},{2,4},{3,12},{4,5},{5,13},{6,1},{7,9},{8,10},{9,2},{10... | collective-permute-start | bytes 393224 | tf_op jit(solution)/shard_map/ppermute | solution.py:126
  10.3 23.8 %collective-permute-start.5 = (bf16[4,2,128,128]{3,2,1,0:T(8,128)(2,1)S(1)}, bf16[4,2,128,128]{3,2,1,0:T(8,128)(2,1)S(1)}, u32[]{:S(2)}, u32[]{:S(2)}) collective-permute-start(bf16[4,2,128,128]{3,2,1,0:T(8,128)(2,1)S(1)} %copy-done.2), channel_id=1, source_target_pairs={{0,1},{1,0},{2,3},{3,2},{4,5},{5,4},{6,7},{7,6},{8,9},{9,8},{10,11... | collective-permute-start | bytes 786440 | tf_op jit(solution)/shard_map/ppermute | solution.py:118
  12.4 21.6 %collective-permute-start.7 = (bf16[4,2,128,128]{3,2,1,0:T(8,128)(2,1)S(1)}, bf16[4,2,128,128]{3,2,1,0:T(8,128)(2,1)S(1)}, u32[]{:S(2)}, u32[]{:S(2)}) collective-permute-start(bf16[4,2,128,128]{3,2,1,0:T(8,128)(2,1)S(1)} %collective-permute-done.6.rest_6_), channel_id=1, source_target_pairs={{0,1},{1,0},{2,3},{3,2},{4,5},{5,4},{6,7},{7,6},{8,9},{9,8},{10,11... | collective-permute-start | bytes 786440 | tf_op jit(solution)/shard_map/ppermute | solution.py:118
  12.5 16.3 %collective-permute-start.3 = (bf16[528,128]{1,0:T(8,128)(2,1)S(1)}, bf16[528,128]{1,0:T(8,128)(2,1)S(1)}, u32[]{:S(2)}, u32[]{:S(2)}) collective-permute-start(bf16[528,128]{1,0:T(8,128)(2,1)S(1)} %get-tuple-element.8), channel_id=1, source_target_pairs={{0,8},{1,12},{2,0},{3,4},{4,13},{5,9},{6,5},{7,1},{8,2},{9,6},{10,... | collective-permute-start | bytes 405512 | tf_op jit(solution)/shard_map/ppermute | solution.py:126
  14.9 14.4 %collective-permute-start.2 = (bf16[528,128]{1,0:T(8,128)(2,1)S(1)}, bf16[528,128]{1,0:T(8,128)(2,1)S(1)}, u32[]{:S(2)}, u32[]{:S(2)}) collective-permute-start(bf16[528,128]{1,0:T(8,128)(2,1)S(1)} %get-tuple-element.8), channel_id=1, source_target_pairs={{0,4},{1,0},{2,12},{3,8},{4,1},{5,5},{6,9},{7,13},{8,14},{9,10},{1... | collective-permute-start | bytes 405512 | tf_op jit(solution)/shard_map/ppermute | solution.py:126
  26.8 7.2 %collective-permute-start.1 = (bf16[528,128]{1,0:T(8,128)(2,1)S(1)}, bf16[528,128]{1,0:T(8,128)(2,1)S(1)}, u32[]{:S(2)}, u32[]{:S(2)}) collective-permute-start(bf16[528,128]{1,0:T(8,128)(2,1)S(1)} %get-tuple-element.8), channel_id=1, source_target_pairs={{0,0},{1,4},{2,8},{3,12},{4,5},{5,1},{6,13},{7,9},{8,10},{9,14},{1... | collective-permute-start | bytes 405512 | tf_op jit(solution)/shard_map/ppermute | solution.py:126

commit v2 on v0

--- a/solution.py
+++ b/solution.py
@@ -1,10 +1,185 @@
+import functools
+
 import jax
 import jax.numpy as jnp
 from jax import lax
+from jax.experimental import pallas as pl
+from jax.experimental.pallas import tpu as pltpu
 from jax.sharding import PartitionSpec as P
 
+ANY = pl.BlockSpec(memory_space=pl.ANY)
+SMEM = pl.BlockSpec(memory_space=pltpu.SMEM)
+VMEM = pl.BlockSpec(memory_space=pltpu.VMEM)
+PARAMS = pltpu.CompilerParams(vmem_limit_bytes=32 * 1024 * 1024)
+ID_ROWS = 16
+
+
+def acting_terms(blocks_ref, sector):
+    first = jnp.int32(0)
+    second = jnp.int32(0)
+    for term in reversed(range(blocks_ref.shape[0])):
+        acts = blocks_ref[term, sector] > 0
+        second = jnp.where(acts, first, second)
+        first = jnp.where(acts, term, first)
+    return first, second
+
+
+def place():
+    op = lax.axis_index("op")
+    return lax.axis_index("blk"), lax.shift_right_logical(op, 1), jnp.bitwise_and(op, 1)
+
+
+def pack_kernel(blocks_ref, psi_ref, left_ref, *rest):
+    outs, sem = list(enumerate(rest[:-1])), rest[-1]
+    z, _, c = place()
+    sectors, tile = psi_ref.shape[0], psi_ref.shape[-1]
+    row = lax.broadcasted_iota(jnp.int32, (ID_ROWS, tile), 0)
+    ids = jnp.zeros((ID_ROWS, tile), jnp.float32)
+    sources = []
+    for local in range(sectors):
+        for slot, term in enumerate(acting_terms(blocks_ref, z * sectors + local)):
+            ids = jnp.where(row == len(sources), term.astype(jnp.float32), ids)
+            sources.append(left_ref.at[term, local])
+    copies = []
+    for step, out in outs:
+        there = jnp.bitwise_xor(z, jnp.bitwise_xor(c, step))
+        column = there * sectors + c
+        blocks = sources + [psi_ref.at[local, column] for local in range(sectors)]
+        for spot, source in enumerate(blocks):
+            copies.append(
+                pltpu.make_async_copy(source, out.at[pl.ds(spot * tile, tile)], sem.at[len(copies)])
+            )
+    for copy in copies:
+        copy.start()
+    for _, out in outs:
+        out[pl.ds(3 * sectors * tile, ID_ROWS)] = ids.astype(jnp.bfloat16)
+    for copy in copies:
+        copy.wait()
+
+
+def apply_kernel(stays, lsize_ref, rsize_ref, *rest):
+    messages, rights, out_ref = rest[:4], rest[4:6], rest[6]
+    z, x, c = place()
+    sectors, tile = out_ref.shape[0], out_ref.shape[-1]
+    terms = rights[0].shape[0]
+    half = lax.shift_right_logical(z, 1)
+    odd = jnp.bitwise_and(z, 1)
+    rows = lax.broadcasted_iota(jnp.int32, (tile, tile), 0)
+    lanes = lax.broadcasted_iota(jnp.int32, (tile, tile), 1)
+
+    def run(far, own_first):
+        owner = 2 * ((1 - half) if far else half) + c
+        pair = messages[2:] if far else messages[:2]
+        order = rights if own_first else rights[::-1]
+        columns = (c, 1 - c) if own_first else (1 - c, c)
+        ids = [ref[pl.ds(3 * sectors * tile, ID_ROWS)].astype(jnp.float32) for ref in pair]
+        for a in range(sectors):
+            height = lsize_ref[owner * sectors + a]
+            cut = []
+            for ref, b in zip(pair, columns):
+                keep = (rows < height) & (lanes < rsize_ref[z * sectors + b])
+                block = ref[pl.ds((2 * sectors + a) * tile, tile)].astype(jnp.float32)
+                cut.append(jnp.where(keep, block, 0.0).astype(jnp.bfloat16))
+            wide = jnp.concatenate(cut, axis=1)
+            applied = []
+            for ref in pair:
+                ops = ref[pl.ds(2 * a * tile, 2 * tile)]
+                both = jnp.dot(ops, wide, preferred_element_type=jnp.float32).astype(jnp.bfloat16)
+                applied += [both[:tile], both[tile:]]
+            for side, b in enumerate(columns):
+                picked = []
+                for s in range(2):
+                    for slot in range(2):
+                        spot = 2 * a + slot
+                        term = jnp.broadcast_to(ids[s][spot : spot + 1], (tile, tile))
+                        block = order[s][0, b].astype(jnp.float32)
+                        for t in range(1, terms):
+                            block = jnp.where(term == t, order[s][t, b].astype(jnp.float32), block)
+                        picked.append(block.astype(jnp.bfloat16))
+                column = [part[:, side * tile : (side + 1) * tile] for part in applied]
+                total = lax.dot_general(
+                    jnp.concatenate(column, axis=1),
+                    jnp.concatenate(picked, axis=1),
+                    (((1,), (1,)), ((), ())),
+                    preferred_element_type=jnp.float32,
+                )
+                out_ref[b, a] = total.astype(out_ref.dtype)
+
+    for far in (False, True):
+        for own_first in (False, True):
+            wanted = ((half == x) != far) == stays
+
+            @pl.when(wanted & (odd == (0 if own_first else 1)))
+            def _(far=far, own_first=own_first):
+                run(far, own_first)
+
+
+def sum_kernel(lsize_ref, rsize_ref, kept_ref, arrived_ref, out_ref):
+    z, _, _ = place()
+    op = lax.axis_index("op")
+    sectors, tile = out_ref.shape[0], out_ref.shape[-1]
+    rows = lax.broadcasted_iota(jnp.int32, (tile, tile), 0)
+    lanes = lax.broadcasted_iota(jnp.int32, (tile, tile), 1)
+    for b in range(sectors):
+        for a in range(sectors):
+            total = kept_ref[b, a] + arrived_ref[b, a].astype(jnp.float32)
+            keep = (rows < lsize_ref[op * sectors + a]) & (lanes < rsize_ref[z * sectors + b])
+            out_ref[b, a] = jnp.where(keep, total, 0.0).astype(jnp.bfloat16)
+
 
 def shards(psi, left_ops, right_ops, term_blocks, left_sizes, right_sizes):
+    n = 4
+    sectors, tile = psi.shape[0], psi.shape[-1]
+    block = functools.partial(jax.ShapeDtypeStruct, dtype=jnp.bfloat16)
+
+    def over_op(array, step):
+        return lax.ppermute(array, "op", [(o, o ^ step) for o in range(n)])
+
+    def over_z(array, distance):
+        pairs = []
+        for z in range(n):
+            for o in range(n):
+                pairs.append((z * n + o, (z ^ distance(o & 1)) * n + (o & 2) + (z & 1)))
+        return lax.ppermute(array, ("blk", "op"), pairs)
+
+    sent = pl.pallas_call(
+        pack_kernel,
+        out_shape=[block((3 * sectors * tile + ID_ROWS, tile))] * n,
+        in_specs=[SMEM, ANY, ANY],
+        out_specs=[VMEM] * n,
+        scratch_shapes=[pltpu.SemaphoreType.DMA((3 * sectors * n,))],
+        compiler_params=pltpu.CompilerParams(vmem_limit_bytes=60 * 1024 * 1024),
+        name="pack",
+    )(term_blocks, psi, left_ops)
+    messages = [None] * n
+    for s in (2, 3, 0, 1):
+        messages[s] = over_z(sent[s], lambda c: s ^ c)
+    held, _ = lax.optimization_barrier((right_ops, sent[0]))
+    rights = [right_ops, over_op(held, 1)]
+
+    def apply(stays, dtype):
+        return pl.pallas_call(
+            functools.partial(apply_kernel, stays),
+            out_shape=jax.ShapeDtypeStruct((sectors, sectors, tile, tile), dtype),
+            in_specs=[SMEM] * 2 + [VMEM] * 6,
+            out_specs=VMEM,
+            compiler_params=PARAMS,
+            name="apply_kept" if stays else "apply_sent",
+        )(left_sizes, right_sizes, *messages, *rights)
+
+    arrived = over_op(apply(False, jnp.bfloat16), 2)
+    kept = apply(True, jnp.float32)
+    return pl.pallas_call(
+        sum_kernel,
+        out_shape=block((sectors, sectors, tile, tile)),
+        in_specs=[SMEM] * 2 + [VMEM] * 2,
+        out_specs=VMEM,
+        compiler_params=PARAMS,
+        name="sum",
+    )(left_sizes, right_sizes, kept, arrived)
+
+
+def wide_shards(psi, left_ops, right_ops, term_blocks, left_sizes, right_sizes):
     sectors_here = psi.shape[0]
     tile_size = psi.shape[2]
     left_first = lax.axis_index("blk") * sectors_here
@@ -50,4 +225,6 @@
         P("parts"),
     )
     out_specs = P(("parts", "blk"), "op", None, None)
-    return jax.shard_map(shards, mesh=mesh, in_specs=in_specs, out_specs=out_specs, check_vma=False)
+    nz, no = mesh.shape["blk"], mesh.shape["op"]
+    body = shards if nz == no == 4 else wide_shards
+    return jax.shard_map(body, mesh=mesh, in_specs=in_specs, out_specs=out_specs, check_vma=False)

time: 89.1 us -> 35.3 us (0.40)
  waiting for transfers between devices: 55.9 us -> 16.5 us
  between operations: 14.1 us -> 0.07 us
  Pallas kernels: 0 us -> 6.83 us
  local copies, waits for them, and re-layouts: 5.63 us -> 0.02 us
  starting transfers between devices: 6.32 us -> 11.5 us
  other arithmetic: 4.02 us -> 0 us
  matrix products: 2.87 us -> 0 us
    unnamed x2 -> x0, waiting for transfers between devices: 31 us -> none
    all_to_all x1 -> x0, waiting for transfers between devices: 24.9 us -> none  [shards(): lax.all_to_all(applied, 'blk', split_axis=2, concat_axis=1, tiled=True)]
    ppermute x0 -> x6, waiting for transfers between devices: none -> 16.5 us  [the longest x4 14.7 us: over_z(): return lax.ppermute(array, ('blk', 'op'), pairs)]
    ppermute x0 -> x6, starting transfers between devices: none -> 11.5 us  [the longest x4 8.73 us: over_z(): return lax.ppermute(array, ('blk', 'op'), pairs)]
    pallas_call x0 -> x4, Pallas kernels: none -> 6.83 us  [the longest x1 3.16 us: shards(): pl.pallas_call(pack_kernel, out_shape=[block((3 * sectors * tile + ID_ROW...]
    all_to_all x1 -> x0, starting transfers between devices: 6.31 us -> none  [shards(): lax.all_to_all(applied, 'blk', split_axis=2, concat_axis=1, tiled=True)]
    dot_general x2 -> x0, matrix products: 2.87 us -> none  [the longest x1 1.62 us: shards(): jnp.einsum('kaim,abmj->kabij', picked, masked, preferred_element_type=jnp...]
    gather x2 -> x0, local copies, waits for them, and re-layouts: 2.27 us -> none  [the longest x1 1.52 us: shards(): picked = left_ops[ids_local, sector_index]]
  transfers between devices with their start and end apart: 2 -> 6, of which waited for: 2 -> 3; matrix products, arithmetic and copies ran while one was open for 2% -> 0% of each run, Pallas kernels for 0% -> 3%
where the time goes in v2:
time: 35.3 us; the launch traced here: 34.9 us
  waiting for transfers between devices  16.5 us (47%)
  starting transfers between devices  11.5 us (33%)
  Pallas kernels  6.83 us (19%)
    ppermute x4, waiting for transfers between devices, over_z(): return lax.ppermute(array, ('blk', 'op'), pairs)  14.7 us
    ppermute x4, starting transfers between devices, over_z(): return lax.ppermute(array, ('blk', 'op'), pairs)  8.73 us
    pallas_call x1, Pallas kernels, shards(): pl.pallas_call(pack_kernel, out_shape=[block((3 * sectors * tile + ID_ROW...  3.16 us
    ppermute x2, starting transfers between devices, over_op(): return lax.ppermute(array, 'op', [(o, o ^ step) for o in range(n)])  2.8 us
    pallas_call x2, Pallas kernels, apply(): pl.pallas_call(functools.partial(apply_kernel, stays), out_shape=jax.Shap...  2.41 us
    ppermute x2, waiting for transfers between devices, over_op(): return lax.ppermute(array, 'op', [(o, o ^ step) for o in range(n)])  1.74 us
    pallas_call x1, Pallas kernels, shards(): pl.pallas_call(sum_kernel, out_shape=block((sectors, sectors, tile, tile)...  1.26 us
  transfers between devices with their start and end apart: 6, of which 3 were waited for; matrix products, arithmetic and copies ran while one was open for 0% of the time, Pallas kernels for 3%

profile of v2, /device:TPU:0, one launch (start us, length us, event | category | flops | bytes accessed | tf_op | source)
XLA Modules:
  0.0 34.9 jit_solution(9671370808068895891)
XLA Ops:
  0.0 0.0 copy-start
  0.0 3.2 %pack.1 = (bf16[784,128]{1,0:T(8,128)(2,1)}, bf16[784,128]{1,0:T(8,128)(2,1)}, bf16[784,128]{1,0:T(8,128)(2,1)}, bf16[784,128]{1,0:T(8,128)(2,1)}) custom-call(s32[4,8]{1,0:T(4,128)} %blocks_ref.1, bf16[2,8,128,128]{3,2,1,0:T(8,128)(2,1)} %psi_ref.1, bf16[4,2,128,128]{3,2,1,0:T(8,128)(2,1)} %left_ref.1), custom_call_target="tpu_custom_call" | custom-call | tf_op jit(solution)/shard_map/pack/pallas_call | solution.py:145
  3.2 0.0 copy-done
  3.2 0.5 %collective-permute-start.4 = (bf16[4,2,128,128]{3,2,1,0:T(8,128)(2,1)S(1)}, bf16[4,2,128,128]{3,2,1,0:T(8,128)(2,1)S(1)}, u32[]{:S(2)}, u32[]{:S(2)}) collective-permute-start(bf16[4,2,128,128]{3,2,1,0:T(8,128)(2,1)S(1)} %copy-done), channel_id=1, source_target_pairs={{0,1},{1,0},{2,3},{3,2},{4,5},{5,4},{6,7},{7,6},{8,9},{9,8},{10,11... | collective-permute-start | bytes 786440 | tf_op jit(solution)/shard_map/ppermute | solution.py:136
  3.7 4.4 %collective-permute-start.1 = (bf16[784,128]{1,0:T(8,128)(2,1)}, bf16[784,128]{1,0:T(8,128)(2,1)S(1)}, u32[]{:S(2)}, u32[]{:S(2)}) collective-permute-start(bf16[784,128]{1,0:T(8,128)(2,1)} %get-tuple-element.11), channel_id=1, source_target_pairs={{0,4},{1,0},{2,6},{3,2},{4,1},{5,5},{6,3},{7,7},{8,12},{9,8},{10,1... | collective-permute-start | bytes 602120 | tf_op jit(solution)/shard_map/ppermute | solution.py:143
  8.1 0.0 copy-start.1
  8.1 0.0 copy-start.2
  8.1 2.7 %collective-permute-start.2 = (bf16[784,128]{1,0:T(8,128)(2,1)}, bf16[784,128]{1,0:T(8,128)(2,1)S(1)}, u32[]{:S(2)}, u32[]{:S(2)}) collective-permute-start(bf16[784,128]{1,0:T(8,128)(2,1)} %get-tuple-element.12), channel_id=1, source_target_pairs={{0,8},{1,12},{2,10},{3,14},{4,13},{5,9},{6,15},{7,11},{8,0},{9,4},... | collective-permute-start | bytes 602120 | tf_op jit(solution)/shard_map/ppermute | solution.py:143
  10.8 0.1 collective-permute-start.3
  10.9 1.6 %collective-permute-start = (bf16[784,128]{1,0:T(8,128)(2,1)}, bf16[784,128]{1,0:T(8,128)(2,1)S(1)}, u32[]{:S(2)}, u32[]{:S(2)}) collective-permute-start(bf16[784,128]{1,0:T(8,128)(2,1)} %get-tuple-element.10), channel_id=1, source_target_pairs={{0,0},{1,4},{2,2},{3,6},{4,5},{5,1},{6,7},{7,3},{8,8},{9,12},{10,1... | collective-permute-start | bytes 602120 | tf_op jit(solution)/shard_map/ppermute | solution.py:143
  12.5 0.0 collective-permute-done.1.rest_1_
  12.5 12.1 %collective-permute-done.2.rest_2_ = bf16[784,128]{1,0:T(8,128)(2,1)S(1)} collective-permute-done((bf16[784,128]{1,0:T(8,128)(2,1)}, bf16[784,128]{1,0:T(8,128)(2,1)S(1)}, u32[]{:S(2)}, u32[]{:S(2)}) %collective-permute-start.2) | collective-permute-done | bytes 200736 | tf_op jit(solution)/shard_map/ppermute | solution.py:143
  24.6 2.6 %collective-permute-done.3.rest_3_ = bf16[784,128]{1,0:T(8,128)(2,1)S(1)} collective-permute-done((bf16[784,128]{1,0:T(8,128)(2,1)}, bf16[784,128]{1,0:T(8,128)(2,1)S(1)}, u32[]{:S(2)}, u32[]{:S(2)}) %collective-permute-start.3) | collective-permute-done | bytes 200736 | tf_op jit(solution)/shard_map/ppermute | solution.py:143
  27.2 0.0 collective-permute-done.rest_0_
  27.2 0.0 collective-permute-done.4.rest_5_
  27.2 0.0 copy-done.1
  27.2 0.0 copy-done.2
  27.2 1.2 %apply_sent.1 = bf16[2,2,128,128]{3,2,1,0:T(8,128)(2,1)S(1)} custom-call(s32[8]{0:T(128)S(1)} %copy-done.1, s32[8]{0:T(128)S(1)} %copy-done.2, bf16[784,128]{1,0:T(8,128)(2,1)S(1)} %collective-permute-done.rest_0_, bf16[784,128]{1,0:T(8,128)(2,1)S(1)} %collective-permute-done.1.rest_1_, bf16[784,128]{1,0:T(8,128)(2,1)S(1)} %collective-permute-done.2.rest_2_, ...), custom_call_target="tpu_custom_call" | custom-call | tf_op jit(solution)/shard_map/apply_sent/pallas_call | solution.py:161
  28.5 2.3 %collective-permute-start.5 = (bf16[2,2,128,128]{3,2,1,0:T(8,128)(2,1)S(1)}, bf16[2,2,128,128]{3,2,1,0:T(8,128)(2,1)S(1)}, u32[]{:S(2)}, u32[]{:S(2)}) collective-permute-start(bf16[2,2,128,128]{3,2,1,0:T(8,128)(2,1)S(1)} %apply_sent.1), channel_id=1, source_target_pairs={{0,2},{1,3},{2,0},{3,1},{4,6},{5,7},{6,4},{7,5},{8,10},{9,11},{10,... | collective-permute-start | bytes 393224 | tf_op jit(solution)/shard_map/ppermute | solution.py:136
  30.7 1.2 %apply_kept.1.kept_ref = f32[2,2,128,128]{3,2,1,0:T(8,128)S(1)} custom-call(s32[8]{0:T(128)S(1)} %copy-done.1, s32[8]{0:T(128)S(1)} %copy-done.2, bf16[784,128]{1,0:T(8,128)(2,1)S(1)} %collective-permute-done.rest_0_, bf16[784,128]{1,0:T(8,128)(2,1)S(1)} %collective-permute-done.1.rest_1_, bf16[784,128]{1,0:T(8,128)(2,1)S(1)} %collective-permute-done.2.rest_2_, ...), custom_call_target="tpu_custom_call" | custom-call | tf_op jit(solution)/shard_map/apply_kept/pallas_call | solution.py:161
  31.9 1.7 %collective-permute-done.5.arrived_ref = bf16[2,2,128,128]{3,2,1,0:T(8,128)(2,1)S(1)} collective-permute-done((bf16[2,2,128,128]{3,2,1,0:T(8,128)(2,1)S(1)}, bf16[2,2,128,128]{3,2,1,0:T(8,128)(2,1)S(1)}, u32[]{:S(2)}, u32[]{:S(2)}) %collective-permute-start.5) | collective-permute-done | bytes 131104 | tf_op jit(solution)/shard_map/ppermute | solution.py:136
  33.7 1.3 %sum.1 = bf16[2,2,128,128]{3,2,1,0:T(8,128)(2,1)} custom-call(s32[8]{0:T(128)S(1)} %copy-done.1, s32[8]{0:T(128)S(1)} %copy-done.2, f32[2,2,128,128]{3,2,1,0:T(8,128)S(1)} %apply_kept.1.kept_ref, bf16[2,2,128,128]{3,2,1,0:T(8,128)(2,1)S(1)} %collective-permute-done.5.arrived_ref), custom_call_target="tpu_custom_call" | custom-call | tf_op jit(solution)/shard_map/sum/pallas_call | solution.py:172
Async XLA Ops:
  0.0 3.2 %copy-start = (bf16[4,2,128,128]{3,2,1,0:T(8,128)(2,1)S(1)}, bf16[4,2,128,128]{3,2,1,0:T(8,128)(2,1)}, u32[]{:S(2)}) copy-start(bf16[4,2,128,128]{3,2,1,0:T(8,128)(2,1)} %rest_4_.3) | copy-start | bytes 786436
  3.2 24.0 %collective-permute-start.4 = (bf16[4,2,128,128]{3,2,1,0:T(8,128)(2,1)S(1)}, bf16[4,2,128,128]{3,2,1,0:T(8,128)(2,1)S(1)}, u32[]{:S(2)}, u32[]{:S(2)}) collective-permute-start(bf16[4,2,128,128]{3,2,1,0:T(8,128)(2,1)S(1)} %copy-done), channel_id=1, source_target_pairs={{0,1},{1,0},{2,3},{3,2},{4,5},{5,4},{6,7},{7,6},{8,9},{9,8},{10,11... | collective-permute-start | bytes 786440 | tf_op jit(solution)/shard_map/ppermute | solution.py:136
  3.7 8.8 %collective-permute-start.1 = (bf16[784,128]{1,0:T(8,128)(2,1)}, bf16[784,128]{1,0:T(8,128)(2,1)S(1)}, u32[]{:S(2)}, u32[]{:S(2)}) collective-permute-start(bf16[784,128]{1,0:T(8,128)(2,1)} %get-tuple-element.11), channel_id=1, source_target_pairs={{0,4},{1,0},{2,6},{3,2},{4,1},{5,5},{6,3},{7,7},{8,12},{9,8},{10,1... | collective-permute-start | bytes 602120 | tf_op jit(solution)/shard_map/ppermute | solution.py:143
  8.1 19.1 %copy-start.1 = (s32[8]{0:T(128)S(1)}, s32[8]{0:T(128)}, u32[]{:S(2)}) copy-start(s32[8]{0:T(128)} %lsize_ref.5) | copy-start | bytes 100
  8.1 19.1 %copy-start.2 = (s32[8]{0:T(128)S(1)}, s32[8]{0:T(128)}, u32[]{:S(2)}) copy-start(s32[8]{0:T(128)} %rsize_ref.5) | copy-start | bytes 100
  8.1 16.4 %collective-permute-start.2 = (bf16[784,128]{1,0:T(8,128)(2,1)}, bf16[784,128]{1,0:T(8,128)(2,1)S(1)}, u32[]{:S(2)}, u32[]{:S(2)}) collective-permute-start(bf16[784,128]{1,0:T(8,128)(2,1)} %get-tuple-element.12), channel_id=1, source_target_pairs={{0,8},{1,12},{2,10},{3,14},{4,13},{5,9},{6,15},{7,11},{8,0},{9,4},... | collective-permute-start | bytes 602120 | tf_op jit(solution)/shard_map/ppermute | solution.py:143
  10.8 16.4 %collective-permute-start.3 = (bf16[784,128]{1,0:T(8,128)(2,1)}, bf16[784,128]{1,0:T(8,128)(2,1)S(1)}, u32[]{:S(2)}, u32[]{:S(2)}) collective-permute-start(bf16[784,128]{1,0:T(8,128)(2,1)} %get-tuple-element.13), channel_id=1, source_target_pairs={{0,12},{1,8},{2,14},{3,10},{4,9},{5,13},{6,11},{7,15},{8,4},{9,0},... | collective-permute-start | bytes 602120 | tf_op jit(solution)/shard_map/ppermute | solution.py:143
  10.9 16.3 %collective-permute-start = (bf16[784,128]{1,0:T(8,128)(2,1)}, bf16[784,128]{1,0:T(8,128)(2,1)S(1)}, u32[]{:S(2)}, u32[]{:S(2)}) collective-permute-start(bf16[784,128]{1,0:T(8,128)(2,1)} %get-tuple-element.10), channel_id=1, source_target_pairs={{0,0},{1,4},{2,2},{3,6},{4,5},{5,1},{6,7},{7,3},{8,8},{9,12},{10,1... | collective-permute-start | bytes 602120 | tf_op jit(solution)/shard_map/ppermute | solution.py:143
  28.5 5.2 %collective-permute-start.5 = (bf16[2,2,128,128]{3,2,1,0:T(8,128)(2,1)S(1)}, bf16[2,2,128,128]{3,2,1,0:T(8,128)(2,1)S(1)}, u32[]{:S(2)}, u32[]{:S(2)}) collective-permute-start(bf16[2,2,128,128]{3,2,1,0:T(8,128)(2,1)S(1)} %apply_sent.1), channel_id=1, source_target_pairs={{0,2},{1,3},{2,0},{3,1},{4,6},{5,7},{6,4},{7,5},{8,10},{9,11},{10,... | collective-permute-start | bytes 393224 | tf_op jit(solution)/shard_map/ppermute | solution.py:136
